TPU v7x, 128 devices: a whole 4x4x4 slice. The times are simulated.
128 devices in a mesh: row: 8 (over x_lo, z), col: 8 (over y, x_hi), depth: 2 (over core).
Axes of the slice: x: 4 (x_hi: 2, x_lo: 2; x = x_hi * 2 + x_lo), y: 4, z: 4, core: 2. Of those that a mesh axis runs over, the one named last changes fastest.
Arguments:
- tokens: bfloat16 [2048, 12288], P('col', ('row', 'depth')), may hold values from -6 to 6
- up_weight: bfloat16 [12288, 24576], P(('row', 'depth'), 'col'), may hold values from -0.0546875 to 0.0546875
- up_bias: float32 [24576], P('col'), may hold values from -3 to 3
- down_weight: bfloat16 [24576, 12288], P('col', ('row', 'depth')), may hold values from -0.0390625 to 0.0390625
- down_bias: float32 [12288], P(('row', 'depth')), may hold values from -3 to 3
Outputs:
- block_output: float32 [2048, 12288], P('col', ('row', 'depth'))
All inputs are finite; a program needn't handle non-finite values.
Results may differ from a plain program's by a relative error of at most 0.0025.
Values may be sent and summed in bfloat16 or wider, within the bound.
No kernel may reach another device: no remote copies, remote signals or barrier semaphores. Data moves between devices by JAX's collectives and lax.ppermute only.
A program may use at most 128 MiB of HBM per device.

v0:
```python
import jax
import jax.numpy as jnp
from jax import lax
from jax.sharding import PartitionSpec as P


def body(tokens, up_weight, up_bias, down_weight, down_bias):
    partial_value = jnp.dot(
        lax.all_gather(tokens, "col", axis=0, tiled=True),
        up_weight,
        preferred_element_type=jnp.float32,
    )
    summed = lax.psum(partial_value, ("row", "depth"))
    activation = jax.nn.gelu(summed + up_bias, approximate=True).astype(jnp.bfloat16)
    output_terms = jnp.dot(activation, down_weight, preferred_element_type=jnp.float32)
    reduced = lax.psum_scatter(output_terms, "col", scatter_dimension=0, tiled=True)
    return reduced + down_bias


def solution(mesh):
    placed = (
        P("col", ("row", "depth")),
        P(("row", "depth"), "col"),
        P("col"),
        P("col", ("row", "depth")),
        P(("row", "depth")),
    )
    return jax.shard_map(
        body, mesh=mesh, in_specs=placed, out_specs=P("col", ("row", "depth")), check_vma=False
    )
```

profile of v0, /device:TPU:1, one launch (start us, length us, event | category | flops | bytes accessed | tf_op | source)
XLA Modules:
  0.0 499.7 jit_solution(5747897183498957607)
XLA Ops:
  6.5 0.0 all-gather.2.cloned.1.call-start
  6.5 0.7 all-gather.2.cloned.1.call-update
  7.3 0.0 all-reduce.2.cloned.1.call-start
  7.3 67.8 %all-gather.2.cloned.1.call-done = bf16[2048,768]{1,0:T(8,128)(2,1)} async-done(((bf16[256,768]{1,0:T(8,128)(2,1)}), bf16[2048,768]{1,0:T(8,128)(2,1)}) %all-gather.2.cloned.1.call-update) | async-done | bytes 3145744 | tf_op jit(solution)/shard_map/all_gather | solution.py:9
  75.1 17.4 %fusion.14 = f32[2048,3072]{1,0:T(8,128)} fusion(bf16[2048,768]{1,0:T(8,128)(2,1)} %all-gather.2.cloned.1.call-done, bf16[768,3072]{1,0:T(8,128)(2,1)} %param.6), kind=kOutput, calls=%fused_computation.15 | convolution fusion | flops 9663676416 | bytes 33030144 | tf_op jit(solution)/shard_map/dot_general | solution.py:8
  92.4 0.0 copy-start.1
  92.4 0.0 all-reduce.2.cloned.1.call-update
  92.5 0.0 copy-start
  92.5 0.0 reduce-scatter.2.cloned.1.call-start
  92.5 277.6 %all-reduce.2.cloned.1.call-done = f32[2048,3072]{1,0:T(8,128)} async-done(((f32[2048,3072]{1,0:T(8,128)}), f32[2048,3072]{1,0:T(8,128)}) %all-reduce.2.cloned.1.call-update) | async-done | bytes 25165840 | tf_op jit(solution)/shard_map/psum | solution.py:13
  370.1 0.0 copy-done.1
  370.1 23.1 %fusion.8 = f32[2048,768]{1,0:T(8,128)} fusion(bf16[3072,768]{1,0:T(8,128)(2,1)} %param.8, f32[2048,3072]{1,0:T(8,128)} %all-reduce.2.cloned.1.call-done, f32[3072]{0:T(1024)S(1)} %copy-done.1), kind=kOutput, calls=%fused_computation.9 | convolution fusion | flops 9726590976 | bytes 36188160 | tf_op jit(solution)/shard_map/dot_general | solution.py:15
  393.3 0.0 reduce-scatter.2.cloned.1.call-update
  393.3 97.9 %reduce-scatter.2.cloned.1.call-done = f32[256,768]{1,0:T(8,128)} async-done(((f32[2048,768]{1,0:T(8,128)}), f32[256,768]{1,0:T(8,128)}) %reduce-scatter.2.cloned.1.call-update) | async-done | bytes 786448 | tf_op jit(solution)/shard_map/reduce_scatter | solution.py:16
  491.1 0.0 copy-done
  491.1 2.1 broadcast_add_fusion
Async XLA Ops:
  6.5 68.5 %all-gather.2.cloned.1.call-start = ((), (), s32[]{:S(2)}) async-start(), calls=%async_computation.1 | async-start | bytes 3538944 | tf_op jit(solution)/shard_map/all_gather | solution.py:9
  7.3 362.9 %all-reduce.2.cloned.1.call-start = ((), (), s32[]{:S(2)}) async-start(), calls=%async_computation.2 | async-start | bytes 50331648 | tf_op jit(solution)/shard_map/psum | solution.py:13
  92.4 277.7 %copy-start.1 = (f32[3072]{0:T(1024)S(1)}, f32[3072]{0:T(1024)}, u32[]{:S(2)}) copy-start(f32[3072]{0:T(1024)} %param.7) | copy-start | bytes 36868
  92.5 398.7 %copy-start = (f32[768]{0:T(1024)S(1)}, f32[768]{0:T(1024)}, u32[]{:S(2)}) copy-start(f32[768]{0:T(1024)} %param.9) | copy-start | bytes 9220
  92.5 398.7 %reduce-scatter.2.cloned.1.call-start = ((), (), s32[]{:S(2)}) async-start(), calls=%async_computation.3 | async-start | bytes 7077888 | tf_op jit(solution)/shard_map/reduce_scatter | solution.py:16
Sparse Core Ops, SparseCore 0:
  9.7 65.3 all-gather.1
  92.6 277.4 all-reduce.1
  393.4 97.6 reduce-scatter.1
where the time goes:
time: 500 us
  waiting for transfers between devices  444 us (89%)
  matrix products  40.5 us (8%)
  between operations  13.1 us (3%)
    psum x1, waiting for transfers between devices, body(): summed = lax.psum(partial_value, ('row', 'depth'))  278 us
    reduce_scatter x1, waiting for transfers between devices, body(): lax.psum_scatter(output_terms, 'col', scatter_dimension=0, tiled=True)  97.9 us
    all_gather x1, waiting for transfers between devices, body(): lax.all_gather(tokens, 'col', axis=0, tiled=True)  67.8 us
    dot_general x1, matrix products, body(): jnp.dot(activation, down_weight, preferred_element_type=jnp.float32)  23.1 us
    dot_general x1, matrix products, body(): jnp.dot(lax.all_gather(tokens, 'col', axis=0, tiled=True), up_weight, pre...  17.4 us
  transfers between devices with their start and end apart: 3, of which 3 were waited for; matrix products, arithmetic and copies ran while one was open for 0% of the time, Pallas kernels for 0%

commit v1 on v0

v1 whole, which is shorter than its diff:
```python
import jax
import jax.numpy as jnp
from jax import lax
from jax.sharding import PartitionSpec as P

BF, F16, F32 = jnp.bfloat16, jnp.float16, jnp.float32
SCALE = 16.0

ROW = {
    "x": [(i, i ^ 8) for i in range(16)],
    "p": [(i, i ^ (6 if i & 1 else 2)) for i in range(16)],
    "q": [(i, i ^ (2 if i & 1 else 6)) for i in range(16)],
}
COL = {
    "x": [(i, i ^ 2) for i in range(16)],
    "p": [(i, i ^ (12 if i & 1 else 4)) for i in range(16)],
    "q": [(i, i ^ (4 if i & 1 else 12)) for i in range(16)],
}
SWAP = [(0, 1), (1, 0)]

UNITS = (3, 3, 2)
LAYOUTS = ('pxq', 'pxq', 'pxq')
TOKEN_ORDER, OUT_ORDER = "xpq", "pqx"
ORDER = tuple(map(int, "013201012302102102010121202130102120212102"))


def row_swap(v, d):
    return lax.ppermute(v, ("row", "depth"), ROW[d])


def col_swap(v, d):
    return lax.ppermute(v, ("col", "depth"), COL[d])


class Chain:
    def __init__(self, token):
        self.token = token

    def after(self, *values):
        *values, self.token = lax.optimization_barrier((*values, self.token))
        return values[0] if len(values) == 1 else values


def chunk(chain, piece, up, up_bias, down, flip, layout, results):
    u, k = piece.shape
    held, dims = chain.after(piece), ""
    for d in TOKEN_ORDER:
        other = col_swap(chain.after(held), d)
        yield
        held, other = chain.after(held, other)
        new = "".join(c for c in layout if c in dims + d)
        at = new.index(d)
        shape = (2**at, held.shape[0] // 2**at, k)
        mine, theirs = held.reshape(shape), other.reshape(shape)
        low = jnp.where(flip[d], theirs, mine)
        high = jnp.where(flip[d], mine, theirs)
        held = chain.after(jnp.stack([low, high], 1).reshape(-1, k))
        dims = new
    half = k // 2
    partial = jnp.dot(held[:, :half], up[0], preferred_element_type=F32)
    partial = SCALE * (partial + jnp.dot(held[:, half:], up[1], preferred_element_type=F32))
    rows = partial.shape[0] // 2
    held, send = partial[:rows], partial[rows:].astype(F16)
    for d in layout:
        if d != layout[0]:
            rows = held.shape[0] // 2
            send, held = held[rows:], held[:rows]
        send, held = chain.after(send.astype(F16), held)
        got = row_swap(send, d)
        yield
        held, got = chain.after(held, got)
        held = held + got.astype(F32)
    held = jax.nn.gelu(held * (1 / SCALE) + up_bias, approximate=True).astype(BF)
    for d in reversed(layout):
        other = row_swap(chain.after(held), d)
        yield
        held, other = chain.after(held, other)
        held = chain.after(jnp.concatenate([held, other], 0))
    held, dims = jnp.stack([jnp.dot(held, w, preferred_element_type=F32) for w in down]), layout
    for d in OUT_ORDER:
        at, (_, rows, n) = dims.index(d), held.shape
        parts = held.reshape(2, 2**at, 2, rows // 2 ** (at + 1), n)
        low, high = parts[:, :, 0], parts[:, :, 1]
        send = jnp.where(flip[d], low, high).astype(BF).reshape(2, rows // 2, n)
        held = jnp.where(flip[d], high, low).reshape(2, rows // 2, n)
        send, held = chain.after(send, held)
        got = col_swap(send, d)
        yield
        held, got = chain.after(held, got)
        held = held + got.astype(F32)
        dims = dims.replace(d, "")
    results.append(chain.after(held))


def fetch(chain, up, down):
    for w in (up, down):
        other = lax.ppermute(chain.after(w[0]), "depth", SWAP)
        yield
        w.append(chain.after(jnp.where(chain.token, chain.after(other), jnp.zeros_like(other))))


def body(tokens, up_weight, up_bias, down_weight, down_bias):
    row, col, depth = (lax.axis_index(a) for a in ("row", "col", "depth"))
    zy = (row % 4) ^ (col // 2)
    b_bit = zy // 2
    a_bit = (zy % 2) ^ b_bit
    flip = {
        "x": ((row // 4) ^ (col % 2)) == 1,
        "p": jnp.where(depth == 0, a_bit, b_bit) == 1,
        "q": jnp.where(depth == 0, b_bit, a_bit) == 1,
    }
    half = tokens.shape[0] // 2

    give = lax.dynamic_slice_in_dim(tokens, (1 - depth) * half, half, 0)
    keep = lax.dynamic_slice_in_dim(tokens, depth * half, half, 0)
    mine = jnp.concatenate([keep, lax.ppermute(give, "depth", SWAP)], 1)
    chain = Chain(row < 8)
    up, down = [up_weight], [down_weight]
    weights = fetch(chain, up, down)

    results, steps, at = [[] for _ in UNITS], [], 0
    for units, layout, result in zip(UNITS, LAYOUTS, results):
        piece = mine[at : at + 16 * units]
        steps.append(chunk(chain, piece, up, up_bias, down, flip, layout, result))
        at += 16 * units
    steps.append(weights)
    for i in ORDER:
        next(steps[i], None)
    out = jnp.concatenate([r[0] for r in results], 1)
    own, other = out[0], out[1]
    got = lax.ppermute(other, "depth", SWAP)
    first = jnp.where(depth == 0, own, got)
    last = jnp.where(depth == 0, got, own)
    return jnp.where(chain.token, jnp.concatenate([first, last], 0) + down_bias, 0.0)


def solution(mesh):
    placed = (
        P("col", ("row", "depth")),
        P(("row", "depth"), "col"),
        P("col"),
        P("col", ("row", "depth")),
        P(("row", "depth")),
    )
    return jax.shard_map(
        body, mesh=mesh, in_specs=placed, out_specs=P("col", ("row", "depth")), check_vma=False
    )
```

time: 500 us -> 187 us (0.37)
  waiting for transfers between devices: 444 us -> 77.1 us
  starting transfers between devices: 0.08 us -> 73.5 us
  matrix products: 40.5 us -> 22.1 us
  between operations: 13.1 us -> 0.81 us
  other arithmetic: 2.06 us -> 11.1 us
    psum x1 -> x0, waiting for transfers between devices: 278 us -> none  [body(): summed = lax.psum(partial_value, ('row', 'depth'))]
    reduce_scatter x1 -> x0, waiting for transfers between devices: 97.9 us -> none  [body(): lax.psum_scatter(output_terms, 'col', scatter_dimension=0, tiled=True)]
    ppermute x0 -> x40, waiting for transfers between devices: none -> 77.1 us  [the longest x18 51.2 us: row_swap(): return lax.ppermute(v, ('row', 'depth'), ROW[d])]
    ppermute x0 -> x40, starting transfers between devices: none -> 73.5 us  [the longest x18 33 us: row_swap(): return lax.ppermute(v, ('row', 'depth'), ROW[d])]
    all_gather x1 -> x0, waiting for transfers between devices: 67.8 us -> none  [body(): lax.all_gather(tokens, 'col', axis=0, tiled=True)]
    dot_general x2 -> x12, matrix products: 40.5 us -> 22.1 us  [the longest x6 10.9 us: chunk(): jnp.dot(held, w, preferred_element_type=F32)]
  transfers between devices with their start and end apart: 3 -> 40, of which waited for: 3 -> 24; matrix products, arithmetic and copies ran while one was open for 0% -> 17% of each run, Pallas kernels for 0% -> 0%
where the time goes in v1:
time: 187 us; the launch traced here: 186 us
  waiting for transfers between devices  77.1 us (41%)
  starting transfers between devices  73.5 us (39%)
  matrix products  22.1 us (12%)
  other arithmetic  11.1 us (6%)
    ppermute x18, waiting for transfers between devices, row_swap(): return lax.ppermute(v, ('row', 'depth'), ROW[d])  51.2 us
    ppermute x18, starting transfers between devices, row_swap(): return lax.ppermute(v, ('row', 'depth'), ROW[d])  33 us
    ppermute x18, starting transfers between devices, col_swap(): return lax.ppermute(v, ('col', 'depth'), COL[d])  31.4 us
    ppermute x18, waiting for transfers between devices, col_swap(): return lax.ppermute(v, ('col', 'depth'), COL[d])  23.5 us
    dot_general x6, matrix products, chunk(): jnp.dot(held, w, preferred_element_type=F32)  10.9 us
    dot_general x3, matrix products, chunk(): jnp.dot(held[:, half:], up[1], preferred_element_type=F32)  5.66 us
    dot_general x3, matrix products, chunk(): partial = jnp.dot(held[:, :half], up[0], preferred_element_type=F32)  5.47 us
    ppermute x1, starting transfers between devices, body(): got = lax.ppermute(other, 'depth', SWAP)  5.35 us
  transfers between devices with their start and end apart: 40, of which 24 were waited for; matrix products, arithmetic and copies ran while one was open for 17% of the time, Pallas kernels for 0%

profile of v1, /device:TPU:1, one launch (start us, length us, event | category | flops | bytes accessed | tf_op | source)
XLA Modules:
  0.0 185.8 jit_solution(891068396449386159)
XLA Ops:
  4.1 2.8 %collective-permute-start.3 = (bf16[48,1536]{1,0:T(8,128)(2,1)S(1)}, bf16[48,1536]{1,0:T(8,128)(2,1)S(1)}, u32[]{:S(2)}, u32[]{:S(2)}) collective-permute-start(bf16[48,1536]{1,0:T(8,128)(2,1)S(1)} %get-tuple-element.259), channel_id=1, source_target_pairs={{0,2},{1,3},{2,0},{3,1},{4,6},{5,7},{6,4},{7,5},{8,10},{9,11},{10,... | collective-permute-start | bytes 442376 | tf_op jit(solution)/shard_map/ppermute | solution.py:32
  7.2 2.8 %collective-permute-start.1 = (bf16[32,1536]{1,0:T(8,128)(2,1)S(1)}, bf16[32,1536]{1,0:T(8,128)(2,1)S(1)}, u32[]{:S(2)}, u32[]{:S(2)}) collective-permute-start(bf16[32,1536]{1,0:T(8,128)(2,1)S(1)} %pad_maximum_fusion.23), channel_id=1, source_target_pairs={{0,2},{1,3},{2,0},{3,1},{4,6},{5,7},{6,4},{7,5},{8,10},{9,11},{10,... | collective-permute-start | bytes 294920 | tf_op jit(solution)/shard_map/ppermute | solution.py:32
  11.0 2.9 %collective-permute-start.5 = (bf16[96,1536]{1,0:T(8,128)(2,1)S(1)}, bf16[96,1536]{1,0:T(8,128)(2,1)S(1)}, u32[]{:S(2)}, u32[]{:S(2)}) collective-permute-start(bf16[96,1536]{1,0:T(8,128)(2,1)S(1)} %bitcast.266), channel_id=1, source_target_pairs={{0,4},{1,13},{2,6},{3,15},{4,0},{5,9},{6,2},{7,11},{8,12},{9,5},{1... | collective-permute-start | bytes 884744 | tf_op jit(solution)/shard_map/ppermute | solution.py:32
  14.0 3.0 %collective-permute-start.4 = (bf16[96,1536]{1,0:T(8,128)(2,1)S(1)}, bf16[96,1536]{1,0:T(8,128)(2,1)S(1)}, u32[]{:S(2)}, u32[]{:S(2)}) collective-permute-start(bf16[96,1536]{1,0:T(8,128)(2,1)S(1)} %bitcast.268), channel_id=1, source_target_pairs={{0,4},{1,13},{2,6},{3,15},{4,0},{5,9},{6,2},{7,11},{8,12},{9,5},{1... | collective-permute-start | bytes 884744 | tf_op jit(solution)/shard_map/ppermute | solution.py:32
  18.5 2.7 %collective-permute-done.4 = bf16[96,1536]{1,0:T(8,128)(2,1)S(1)} collective-permute-done((bf16[96,1536]{1,0:T(8,128)(2,1)S(1)}, bf16[96,1536]{1,0:T(8,128)(2,1)S(1)}, u32[]{:S(2)}, u32[]{:S(2)}) %collective-permute-start.4) | collective-permute-done | bytes 294944 | tf_op jit(solution)/shard_map/ppermute | solution.py:32
  33.3 3.8 %collective-permute-start.10 = (f16[192,3072]{1,0:T(8,128)(2,1)S(1)}, f16[192,3072]{1,0:T(8,128)(2,1)S(1)}, u32[]{:S(2)}, u32[]{:S(2)}) collective-permute-start(f16[192,3072]{1,0:T(8,128)(2,1)S(1)} %get-tuple-element.304), channel_id=1, source_target_pairs={{0,16},{1,49},{16,0},{17,33},{32,48},{33,17},{48,32},{49,1},{64,80... | collective-permute-start | bytes 3538952 | tf_op jit(solution)/shard_map/ppermute | solution.py:28
  42.1 3.5 %collective-permute-start.14 = (f16[192,3072]{1,0:T(8,128)(2,1)S(1)}, f16[192,3072]{1,0:T(8,128)(2,1)S(1)}, u32[]{:S(2)}, u32[]{:S(2)}) collective-permute-start(f16[192,3072]{1,0:T(8,128)(2,1)S(1)} %get-tuple-element.328), channel_id=1, source_target_pairs={{0,16},{1,49},{16,0},{17,33},{32,48},{33,17},{48,32},{49,1},{64,80... | collective-permute-start | bytes 3538952 | tf_op jit(solution)/shard_map/ppermute | solution.py:28
  56.0 7.3 %collective-permute-done.14 = f16[192,3072]{1,0:T(8,128)(2,1)S(1)} collective-permute-done((f16[192,3072]{1,0:T(8,128)(2,1)S(1)}, f16[192,3072]{1,0:T(8,128)(2,1)S(1)}, u32[]{:S(2)}, u32[]{:S(2)}) %collective-permute-start.14) | collective-permute-done | bytes 1179680 | tf_op jit(solution)/shard_map/ppermute | solution.py:28
  63.8 2.8 %collective-permute-start.12 = (f16[128,3072]{1,0:T(8,128)(2,1)S(1)}, f16[128,3072]{1,0:T(8,128)(2,1)S(1)}, u32[]{:S(2)}, u32[]{:S(2)}) collective-permute-start(f16[128,3072]{1,0:T(8,128)(2,1)S(1)} %get-tuple-element.324), channel_id=1, source_target_pairs={{0,16},{1,49},{16,0},{17,33},{32,48},{33,17},{48,32},{49,1},{64,80... | collective-permute-start | bytes 2359304 | tf_op jit(solution)/shard_map/ppermute | solution.py:28
  68.2 9.1 %collective-permute-done.12 = f16[128,3072]{1,0:T(8,128)(2,1)S(1)} collective-permute-done((f16[128,3072]{1,0:T(8,128)(2,1)S(1)}, f16[128,3072]{1,0:T(8,128)(2,1)S(1)}, u32[]{:S(2)}, u32[]{:S(2)}) %collective-permute-start.12) | collective-permute-done | bytes 786464 | tf_op jit(solution)/shard_map/ppermute | solution.py:28
  82.3 4.1 %collective-permute-done.19 = bf16[48,3072]{1,0:T(8,128)(2,1)S(1)} collective-permute-done((bf16[48,3072]{1,0:T(8,128)(2,1)S(1)}, bf16[48,3072]{1,0:T(8,128)(2,1)S(1)}, u32[]{:S(2)}, u32[]{:S(2)}) %collective-permute-start.19) | collective-permute-done | bytes 294944 | tf_op jit(solution)/shard_map/ppermute | solution.py:28
  91.6 4.2 %collective-permute-done.21 = bf16[48,3072]{1,0:T(8,128)(2,1)S(1)} collective-permute-done((bf16[48,3072]{1,0:T(8,128)(2,1)S(1)}, bf16[48,3072]{1,0:T(8,128)(2,1)S(1)}, u32[]{:S(2)}, u32[]{:S(2)}) %collective-permute-start.21) | collective-permute-done | bytes 294944 | tf_op jit(solution)/shard_map/ppermute | solution.py:28
  98.8 3.9 %collective-permute-start.25 = (bf16[192,3072]{1,0:T(8,128)(2,1)S(1)}, bf16[192,3072]{1,0:T(8,128)(2,1)S(1)}, u32[]{:S(2)}, u32[]{:S(2)}) collective-permute-start(bf16[192,3072]{1,0:T(8,128)(2,1)S(1)} %pad_maximum_fusion.7), channel_id=1, source_target_pairs={{0,16},{1,49},{16,0},{17,33},{32,48},{33,17},{48,32},{49,1},{64,80... | collective-permute-start | bytes 3538952 | tf_op jit(solution)/shard_map/ppermute | solution.py:28
  105.0 4.1 %collective-permute-done.26 = bf16[96,3072]{1,0:T(8,128)(2,1)S(1)} collective-permute-done((bf16[96,3072]{1,0:T(8,128)(2,1)S(1)}, bf16[96,3072]{1,0:T(8,128)(2,1)S(1)}, u32[]{:S(2)}, u32[]{:S(2)}) %collective-permute-start.26) | collective-permute-done | bytes 589856 | tf_op jit(solution)/shard_map/ppermute | solution.py:28
  109.1 5.4 %collective-permute-start.29 = (bf16[192,3072]{1,0:T(8,128)(2,1)S(1)}, bf16[192,3072]{1,0:T(8,128)(2,1)S(1)}, u32[]{:S(2)}, u32[]{:S(2)}) collective-permute-start(bf16[192,3072]{1,0:T(8,128)(2,1)S(1)} %pad_maximum_fusion.8), channel_id=1, source_target_pairs={{0,16},{1,49},{16,0},{17,33},{32,48},{33,17},{48,32},{49,1},{64,80... | collective-permute-start | bytes 3538952 | tf_op jit(solution)/shard_map/ppermute | solution.py:28
  114.8 4.9 %collective-permute-done.25 = bf16[192,3072]{1,0:T(8,128)(2,1)S(1)} collective-permute-done((bf16[192,3072]{1,0:T(8,128)(2,1)S(1)}, bf16[192,3072]{1,0:T(8,128)(2,1)S(1)}, u32[]{:S(2)}, u32[]{:S(2)}) %collective-permute-start.25) | collective-permute-done | bytes 1179680 | tf_op jit(solution)/shard_map/ppermute | solution.py:28
  124.2 3.2 %collective-permute-start.28 = (bf16[2,192,768]{2,1,0:T(8,128)(2,1)S(1)}, bf16[2,192,768]{2,1,0:T(8,128)(2,1)S(1)}, u32[]{:S(2)}, u32[]{:S(2)}) collective-permute-start(bf16[2,192,768]{2,1,0:T(8,128)(2,1)S(1)} %fusion.24), channel_id=1, source_target_pairs={{0,4},{1,13},{2,6},{3,15},{4,0},{5,9},{6,2},{7,11},{8,12},{9,5},{1... | collective-permute-start | bytes 1769480 | tf_op jit(solution)/shard_map/ppermute | solution.py:32
  127.4 4.9 %collective-permute-done.29 = bf16[192,3072]{1,0:T(8,128)(2,1)S(1)} collective-permute-done((bf16[192,3072]{1,0:T(8,128)(2,1)S(1)}, bf16[192,3072]{1,0:T(8,128)(2,1)S(1)}, u32[]{:S(2)}, u32[]{:S(2)}) %collective-permute-start.29) | collective-permute-done | bytes 1179680 | tf_op jit(solution)/shard_map/ppermute | solution.py:28
  136.9 3.2 %collective-permute-start.31 = (bf16[2,192,768]{2,1,0:T(8,128)(2,1)S(1)}, bf16[2,192,768]{2,1,0:T(8,128)(2,1)S(1)}, u32[]{:S(2)}, u32[]{:S(2)}) collective-permute-start(bf16[2,192,768]{2,1,0:T(8,128)(2,1)S(1)} %fusion.23), channel_id=1, source_target_pairs={{0,4},{1,13},{2,6},{3,15},{4,0},{5,9},{6,2},{7,11},{8,12},{9,5},{1... | collective-permute-start | bytes 1769480 | tf_op jit(solution)/shard_map/ppermute | solution.py:32
  143.1 4.3 %collective-permute-done.31 = bf16[2,192,768]{2,1,0:T(8,128)(2,1)S(1)} collective-permute-done((bf16[2,192,768]{2,1,0:T(8,128)(2,1)S(1)}, bf16[2,192,768]{2,1,0:T(8,128)(2,1)S(1)}, u32[]{:S(2)}, u32[]{:S(2)}) %collective-permute-start.31) | collective-permute-done | bytes 589856 | tf_op jit(solution)/shard_map/ppermute | solution.py:32
  147.7 4.9 %collective-permute-done.30 = bf16[128,3072]{1,0:T(8,128)(2,1)S(1)} collective-permute-done((bf16[128,3072]{1,0:T(8,128)(2,1)S(1)}, bf16[128,3072]{1,0:T(8,128)(2,1)S(1)}, u32[]{:S(2)}, u32[]{:S(2)}) %collective-permute-start.30) | collective-permute-done | bytes 786464 | tf_op jit(solution)/shard_map/ppermute | solution.py:28
  156.3 3.1 %collective-permute-start.37 = (bf16[2,48,768]{2,1,0:T(8,128)(2,1)S(1)}, bf16[2,48,768]{2,1,0:T(8,128)(2,1)S(1)}, u32[]{:S(2)}, u32[]{:S(2)}) collective-permute-start(bf16[2,48,768]{2,1,0:T(8,128)(2,1)S(1)} %fusion.50), channel_id=1, source_target_pairs={{0,2},{1,3},{2,0},{3,1},{4,6},{5,7},{6,4},{7,5},{8,10},{9,11},{10,... | collective-permute-start | bytes 442376 | tf_op jit(solution)/shard_map/ppermute | solution.py:32
  159.4 7.5 %collective-permute-done.32 = bf16[2,128,768]{2,1,0:T(8,128)(2,1)S(1)} collective-permute-done((bf16[2,128,768]{2,1,0:T(8,128)(2,1)S(1)}, bf16[2,128,768]{2,1,0:T(8,128)(2,1)S(1)}, u32[]{:S(2)}, u32[]{:S(2)}) %collective-permute-start.32) | collective-permute-done | bytes 393248 | tf_op jit(solution)/shard_map/ppermute | solution.py:32
  178.1 5.4 %collective-permute-start.39 = (f32[128,768]{1,0:T(8,128)S(1)}, f32[128,768]{1,0:T(8,128)S(1)}, u32[]{:S(2)}, u32[]{:S(2)}) collective-permute-start(f32[128,768]{1,0:T(8,128)S(1)} %slice_bitcast_fusion.4), channel_id=1, source_target_pairs={{0,1},{1,0},{2,3},{3,2},{4,5},{5,4},{6,7},{7,6},{8,9},{9,8},{10,11... | collective-permute-start | bytes 1179656 | tf_op jit(solution)/shard_map/ppermute | solution.py:131
  (165 shorter events, 81.4 us)
Async XLA Ops:
  3.6 20.5 %collective-permute-start.8 = (bf16[768,3072]{1,0:T(8,128)(2,1)}, bf16[768,3072]{1,0:T(8,128)(2,1)}, u32[]{:S(2)}, u32[]{:S(2)}) collective-permute-start(bf16[768,3072]{1,0:T(8,128)(2,1)} %param.6), channel_id=1, source_target_pairs={{0,1},{1,0},{2,3},{3,2},{4,5},{5,4},{6,7},{7,6},{8,9},{9,8},{10,11... | collective-permute-start | bytes 14155784 | tf_op jit(solution)/shard_map/ppermute | solution.py:97
  7.2 14.1 %collective-permute-start.1 = (bf16[32,1536]{1,0:T(8,128)(2,1)S(1)}, bf16[32,1536]{1,0:T(8,128)(2,1)S(1)}, u32[]{:S(2)}, u32[]{:S(2)}) collective-permute-start(bf16[32,1536]{1,0:T(8,128)(2,1)S(1)} %pad_maximum_fusion.23), channel_id=1, source_target_pairs={{0,2},{1,3},{2,0},{3,1},{4,6},{5,7},{6,4},{7,5},{8,10},{9,11},{10,... | collective-permute-start | bytes 294920 | tf_op jit(solution)/shard_map/ppermute | solution.py:32
  21.3 15.8 %collective-permute-start.11 = (bf16[192,1536]{1,0:T(8,128)(2,1)S(1)}, bf16[192,1536]{1,0:T(8,128)(2,1)S(1)}, u32[]{:S(2)}, u32[]{:S(2)}) collective-permute-start(bf16[192,1536]{1,0:T(8,128)(2,1)S(1)} %bitcast.251), channel_id=1, source_target_pairs={{0,12},{1,5},{2,14},{3,7},{4,8},{5,1},{6,10},{7,3},{8,4},{9,13},{1... | collective-permute-start | bytes 1769480 | tf_op jit(solution)/shard_map/ppermute | solution.py:32
  21.7 15.4 %collective-permute-start.6 = (bf16[64,1536]{1,0:T(8,128)(2,1)S(1)}, bf16[64,1536]{1,0:T(8,128)(2,1)S(1)}, u32[]{:S(2)}, u32[]{:S(2)}) collective-permute-start(bf16[64,1536]{1,0:T(8,128)(2,1)S(1)} %bitcast.270), channel_id=1, source_target_pairs={{0,4},{1,13},{2,6},{3,15},{4,0},{5,9},{6,2},{7,11},{8,12},{9,5},{1... | collective-permute-start | bytes 589832 | tf_op jit(solution)/shard_map/ppermute | solution.py:32
  33.3 17.7 %collective-permute-start.10 = (f16[192,3072]{1,0:T(8,128)(2,1)S(1)}, f16[192,3072]{1,0:T(8,128)(2,1)S(1)}, u32[]{:S(2)}, u32[]{:S(2)}) collective-permute-start(f16[192,3072]{1,0:T(8,128)(2,1)S(1)} %get-tuple-element.304), channel_id=1, source_target_pairs={{0,16},{1,49},{16,0},{17,33},{32,48},{33,17},{48,32},{49,1},{64,80... | collective-permute-start | bytes 3538952 | tf_op jit(solution)/shard_map/ppermute | solution.py:28
  42.1 21.2 %collective-permute-start.14 = (f16[192,3072]{1,0:T(8,128)(2,1)S(1)}, f16[192,3072]{1,0:T(8,128)(2,1)S(1)}, u32[]{:S(2)}, u32[]{:S(2)}) collective-permute-start(f16[192,3072]{1,0:T(8,128)(2,1)S(1)} %get-tuple-element.328), channel_id=1, source_target_pairs={{0,16},{1,49},{16,0},{17,33},{32,48},{33,17},{48,32},{49,1},{64,80... | collective-permute-start | bytes 3538952 | tf_op jit(solution)/shard_map/ppermute | solution.py:28
  47.0 67.5 %collective-permute-start.27 = (bf16[3072,768]{1,0:T(8,128)(2,1)S(1)}, bf16[3072,768]{1,0:T(8,128)(2,1)S(1)}, u32[]{:S(2)}, u32[]{:S(2)}) collective-permute-start(bf16[3072,768]{1,0:T(8,128)(2,1)S(1)} %bitcast.278), channel_id=1, source_target_pairs={{0,1},{1,0},{2,3},{3,2},{4,5},{5,4},{6,7},{7,6},{8,9},{9,8},{10,11... | collective-permute-start | bytes 14155784 | tf_op jit(solution)/shard_map/ppermute | solution.py:97
  51.5 16.3 %collective-permute-start.13 = (f16[96,3072]{1,0:T(8,128)(2,1)S(1)}, f16[96,3072]{1,0:T(8,128)(2,1)S(1)}, u32[]{:S(2)}, u32[]{:S(2)}) collective-permute-start(f16[96,3072]{1,0:T(8,128)(2,1)S(1)} %get-tuple-element.326), channel_id=1, source_target_pairs={{0,64},{1,65},{16,80},{17,81},{32,96},{33,97},{48,112},{49,113},{6... | collective-permute-start | bytes 1769480 | tf_op jit(solution)/shard_map/ppermute | solution.py:28
  63.8 13.4 %collective-permute-start.12 = (f16[128,3072]{1,0:T(8,128)(2,1)S(1)}, f16[128,3072]{1,0:T(8,128)(2,1)S(1)}, u32[]{:S(2)}, u32[]{:S(2)}) collective-permute-start(f16[128,3072]{1,0:T(8,128)(2,1)S(1)} %get-tuple-element.324), channel_id=1, source_target_pairs={{0,16},{1,49},{16,0},{17,33},{32,48},{33,17},{48,32},{49,1},{64,80... | collective-permute-start | bytes 2359304 | tf_op jit(solution)/shard_map/ppermute | solution.py:28
  66.6 14.0 %collective-permute-start.16 = (f16[96,3072]{1,0:T(8,128)(2,1)S(1)}, f16[96,3072]{1,0:T(8,128)(2,1)S(1)}, u32[]{:S(2)}, u32[]{:S(2)}) collective-permute-start(f16[96,3072]{1,0:T(8,128)(2,1)S(1)} %get-tuple-element.344), channel_id=1, source_target_pairs={{0,64},{1,65},{16,80},{17,81},{32,96},{33,97},{48,112},{49,113},{6... | collective-permute-start | bytes 1769480 | tf_op jit(solution)/shard_map/ppermute | solution.py:28
  68.1 12.1 %collective-permute-start.17 = (f16[48,3072]{1,0:T(8,128)(2,1)S(1)}, f16[48,3072]{1,0:T(8,128)(2,1)S(1)}, u32[]{:S(2)}, u32[]{:S(2)}) collective-permute-start(f16[48,3072]{1,0:T(8,128)(2,1)S(1)} %get-tuple-element.346), channel_id=1, source_target_pairs={{0,48},{1,17},{16,32},{17,1},{32,16},{33,49},{48,0},{49,33},{64,11... | collective-permute-start | bytes 884744 | tf_op jit(solution)/shard_map/ppermute | solution.py:28
  77.6 12.3 %collective-permute-start.15 = (f16[64,3072]{1,0:T(8,128)(2,1)S(1)}, f16[64,3072]{1,0:T(8,128)(2,1)S(1)}, u32[]{:S(2)}, u32[]{:S(2)}) collective-permute-start(f16[64,3072]{1,0:T(8,128)(2,1)S(1)} %get-tuple-element.342), channel_id=1, source_target_pairs={{0,64},{1,65},{16,80},{17,81},{32,96},{33,97},{48,112},{49,113},{6... | collective-permute-start | bytes 1179656 | tf_op jit(solution)/shard_map/ppermute | solution.py:28
  86.5 12.2 %collective-permute-start.23 = (bf16[96,3072]{1,0:T(8,128)(2,1)S(1)}, bf16[96,3072]{1,0:T(8,128)(2,1)S(1)}, u32[]{:S(2)}, u32[]{:S(2)}) collective-permute-start(bf16[96,3072]{1,0:T(8,128)(2,1)S(1)} %pad_maximum_fusion.14), channel_id=1, source_target_pairs={{0,64},{1,65},{16,80},{17,81},{32,96},{33,97},{48,112},{49,113},{6... | collective-permute-start | bytes 1769480 | tf_op jit(solution)/shard_map/ppermute | solution.py:28
  98.1 10.9 %collective-permute-start.26 = (bf16[96,3072]{1,0:T(8,128)(2,1)S(1)}, bf16[96,3072]{1,0:T(8,128)(2,1)S(1)}, u32[]{:S(2)}, u32[]{:S(2)}) collective-permute-start(bf16[96,3072]{1,0:T(8,128)(2,1)S(1)} %pad_maximum_fusion.15), channel_id=1, source_target_pairs={{0,64},{1,65},{16,80},{17,81},{32,96},{33,97},{48,112},{49,113},{6... | collective-permute-start | bytes 1769480 | tf_op jit(solution)/shard_map/ppermute | solution.py:28
  98.8 20.9 %collective-permute-start.25 = (bf16[192,3072]{1,0:T(8,128)(2,1)S(1)}, bf16[192,3072]{1,0:T(8,128)(2,1)S(1)}, u32[]{:S(2)}, u32[]{:S(2)}) collective-permute-start(bf16[192,3072]{1,0:T(8,128)(2,1)S(1)} %pad_maximum_fusion.7), channel_id=1, source_target_pairs={{0,16},{1,49},{16,0},{17,33},{32,48},{33,17},{48,32},{49,1},{64,80... | collective-permute-start | bytes 3538952 | tf_op jit(solution)/shard_map/ppermute | solution.py:28
  103.5 36.9 %collective-permute-start.24 = (bf16[64,3072]{1,0:T(8,128)(2,1)S(1)}, bf16[64,3072]{1,0:T(8,128)(2,1)S(1)}, u32[]{:S(2)}, u32[]{:S(2)}) collective-permute-start(bf16[64,3072]{1,0:T(8,128)(2,1)S(1)} %pad_maximum_fusion.17), channel_id=1, source_target_pairs={{0,64},{1,65},{16,80},{17,81},{32,96},{33,97},{48,112},{49,113},{6... | collective-permute-start | bytes 1179656 | tf_op jit(solution)/shard_map/ppermute | solution.py:28
  109.1 23.2 %collective-permute-start.29 = (bf16[192,3072]{1,0:T(8,128)(2,1)S(1)}, bf16[192,3072]{1,0:T(8,128)(2,1)S(1)}, u32[]{:S(2)}, u32[]{:S(2)}) collective-permute-start(bf16[192,3072]{1,0:T(8,128)(2,1)S(1)} %pad_maximum_fusion.8), channel_id=1, source_target_pairs={{0,16},{1,49},{16,0},{17,33},{32,48},{33,17},{48,32},{49,1},{64,80... | collective-permute-start | bytes 3538952 | tf_op jit(solution)/shard_map/ppermute | solution.py:28
  124.2 15.8 %collective-permute-start.28 = (bf16[2,192,768]{2,1,0:T(8,128)(2,1)S(1)}, bf16[2,192,768]{2,1,0:T(8,128)(2,1)S(1)}, u32[]{:S(2)}, u32[]{:S(2)}) collective-permute-start(bf16[2,192,768]{2,1,0:T(8,128)(2,1)S(1)} %fusion.24), channel_id=1, source_target_pairs={{0,4},{1,13},{2,6},{3,15},{4,0},{5,9},{6,2},{7,11},{8,12},{9,5},{1... | collective-permute-start | bytes 1769480 | tf_op jit(solution)/shard_map/ppermute | solution.py:32
  136.9 10.4 %collective-permute-start.31 = (bf16[2,192,768]{2,1,0:T(8,128)(2,1)S(1)}, bf16[2,192,768]{2,1,0:T(8,128)(2,1)S(1)}, u32[]{:S(2)}, u32[]{:S(2)}) collective-permute-start(bf16[2,192,768]{2,1,0:T(8,128)(2,1)S(1)} %fusion.23), channel_id=1, source_target_pairs={{0,4},{1,13},{2,6},{3,15},{4,0},{5,9},{6,2},{7,11},{8,12},{9,5},{1... | collective-permute-start | bytes 1769480 | tf_op jit(solution)/shard_map/ppermute | solution.py:32
  140.3 15.5 %collective-permute-start.33 = (bf16[2,96,768]{2,1,0:T(8,128)(2,1)S(1)}, bf16[2,96,768]{2,1,0:T(8,128)(2,1)S(1)}, u32[]{:S(2)}, u32[]{:S(2)}) collective-permute-start(bf16[2,96,768]{2,1,0:T(8,128)(2,1)S(1)} %bitcast.273), channel_id=1, source_target_pairs={{0,12},{1,5},{2,14},{3,7},{4,8},{5,1},{6,10},{7,3},{8,4},{9,13},{1... | collective-permute-start | bytes 884744 | tf_op jit(solution)/shard_map/ppermute | solution.py:32
  140.5 12.1 %collective-permute-start.30 = (bf16[128,3072]{1,0:T(8,128)(2,1)S(1)}, bf16[128,3072]{1,0:T(8,128)(2,1)S(1)}, u32[]{:S(2)}, u32[]{:S(2)}) collective-permute-start(bf16[128,3072]{1,0:T(8,128)(2,1)S(1)} %pad_maximum_fusion.11), channel_id=1, source_target_pairs={{0,16},{1,49},{16,0},{17,33},{32,48},{33,17},{48,32},{49,1},{64,80... | collective-permute-start | bytes 2359304 | tf_op jit(solution)/shard_map/ppermute | solution.py:28
  147.6 19.4 %collective-permute-start.35 = (bf16[2,96,768]{2,1,0:T(8,128)(2,1)S(1)}, bf16[2,96,768]{2,1,0:T(8,128)(2,1)S(1)}, u32[]{:S(2)}, u32[]{:S(2)}) collective-permute-start(bf16[2,96,768]{2,1,0:T(8,128)(2,1)S(1)} %bitcast.272), channel_id=1, source_target_pairs={{0,12},{1,5},{2,14},{3,7},{4,8},{5,1},{6,10},{7,3},{8,4},{9,13},{1... | collective-permute-start | bytes 884744 | tf_op jit(solution)/shard_map/ppermute | solution.py:32
  155.8 11.1 %collective-permute-start.32 = (bf16[2,128,768]{2,1,0:T(8,128)(2,1)S(1)}, bf16[2,128,768]{2,1,0:T(8,128)(2,1)S(1)}, u32[]{:S(2)}, u32[]{:S(2)}) collective-permute-start(bf16[2,128,768]{2,1,0:T(8,128)(2,1)S(1)} %fusion.41), channel_id=1, source_target_pairs={{0,4},{1,13},{2,6},{3,15},{4,0},{5,9},{6,2},{7,11},{8,12},{9,5},{1... | collective-permute-start | bytes 1179656 | tf_op jit(solution)/shard_map/ppermute | solution.py:32
  156.3 16.6 %collective-permute-start.37 = (bf16[2,48,768]{2,1,0:T(8,128)(2,1)S(1)}, bf16[2,48,768]{2,1,0:T(8,128)(2,1)S(1)}, u32[]{:S(2)}, u32[]{:S(2)}) collective-permute-start(bf16[2,48,768]{2,1,0:T(8,128)(2,1)S(1)} %fusion.50), channel_id=1, source_target_pairs={{0,2},{1,3},{2,0},{3,1},{4,6},{5,7},{6,4},{7,5},{8,10},{9,11},{10,... | collective-permute-start | bytes 442376 | tf_op jit(solution)/shard_map/ppermute | solution.py:32
  (22 other events, 149.7 us)
